TPU v7x, 32 devices: a whole 2x2x4 slice. The times are simulated.
32 devices in a mesh: farm: 2 (over x), body: 16 (over z, y, core).
Axes of the slice: x: 2, y: 2, z: 4, core: 2. Of those that a mesh axis runs over, the one named last changes fastest.
Arguments:
- incident: float32 [32, 2, 16, 768], P(('farm', 'body')), parts along dimension 0, may hold values from -6 to 6
- self_inverse: float32 [32, 2, 768, 768], P(('farm', 'body')), parts along dimension 0
- cross_blocks: float32 [32, 4, 2, 768, 768], P(('farm', 'body')), parts along dimension 0, may hold values from -0.046875 to 0.046875
- neighbours: int32 [32, 4], P(('farm', 'body')), parts along dimension 0, may hold values from -1 to 15, as said below
- panel_weight: float32 [32, 768], P(('farm', 'body')), parts along dimension 0, may hold values from -0.0546875 to 0.0546875
Outputs:
- sources: float32 [32, 2, 16, 768], P(('farm', 'body')), parts along dimension 0
- farm_force: float32 [2, 2, 16], P('farm'), parts along dimension 0
There are 2 independent parts, one for each index of `farm`. A program takes and returns all parts, laid end to end along the dimension named above; each array names one. Nothing has to cross between parts.
Inputs may be any that keep to these rules, and one draw needn't show every extreme that they name: `neighbours`: each row names distinct bodies other than its own, each within 8 positions of it around the closed loop of 16 bodies; some body names the body exactly 8 positions away.
All inputs are finite; a program needn't handle non-finite values.
Results may differ from a plain program's by a relative error of at most 0.0003.
Values sent between devices are 32-bit elements; how exact they have to be, the bound alone decides.
A program may use at most 128 MiB of HBM per device.

v0:
```python
import functools

import jax
import jax.numpy as jnp
from jax import lax
from jax.experimental import pallas as pl
from jax.experimental.pallas import tpu as pltpu
from jax.sharding import PartitionSpec as P

ITERS = 6
PIECES = 2
FIRST = 1
DIRECT = 2
F32 = jnp.float32
BF16 = jnp.bfloat16


def flip(index, bits):
    bit = 1
    while bit <= bits:
        if bits & bit:
            index = index + bit - 2 * bit * ((index // bit) % 2)
        bit *= 2
    return index


def pieces(panels):
    first = FIRST * panels // 3
    return [(0, first), (first, panels - first)]


def halves(value):
    high = value.astype(BF16)
    return high, (value - high.astype(F32)).astype(BF16)


def put_field(lhs, column, value, heads):
    rows, width = value.shape
    high, low = halves(value)
    high_t = jnp.concatenate([-high[heads:], high[:heads]], axis=0)
    low_t = jnp.concatenate([-low[heads:], low[:heads]], axis=0)
    lhs[0:rows, column : column + width] = high
    lhs[rows : 2 * rows, column : column + width] = low
    lhs[0:rows, column + width : column + 2 * width] = high_t
    lhs[rows : 2 * rows, column + width : column + 2 * width] = low_t


def multiply(lhs, base, depth, high, low, at, rows):
    deep = slice(base, base + depth)
    both = jnp.dot(lhs[:, 0:depth], high[deep, at], preferred_element_type=F32)
    small = jnp.dot(lhs[0:rows, 0:depth], low[deep, at], preferred_element_type=F32)
    return both[:rows] + both[rows:] + small


def kernel(
    bodies, slots, heads, panels,
    neighbours, incident, inverse, blocks, weight,
    out, force,
    stage, inv_high, inv_low, cross_high, cross_low, lhs, product, shares,
    load_sem, send_sem, recv_sem, share_send, share_recv, *buffers,
):
    rows = 2 * heads
    me = lax.axis_index("body")
    depth_z = bodies // 4
    gathered = (buffers[:PIECES], buffers[PIECES:])
    cuts = [slice(start, start + width) for start, width in pieces(panels)]
    widths = [width for _, width in pieces(panels)]
    tiles = [slice(start, start + 256) for start in range(0, panels, 256)]

    def load(index):
        source = inverse.at[0, index] if index < 2 else blocks.at[0, (index - 2) // 2, (index - 2) % 2]
        return pltpu.make_async_copy(source, stage.at[index], load_sem.at[index])

    for index in range(2 + 2 * slots):
        load(index).start()

    barrier = pltpu.get_barrier_semaphore()
    for bits in range(1, bodies):
        pl.semaphore_signal(barrier, inc=1, device_id={"body": flip(me, bits)})

    def split(index, high, low, part, parts):
        load(index).wait()

        @pl.loop(0, panels // 128)
        def _(step):
            at = pl.ds(pl.multiple_of(step * 128, 128), 128)
            upper, lower = halves(stage[index, at, :].T)
            for piece, cut in enumerate(cuts):
                to = parts * cut.start + part * widths[piece]
                high[to : to + widths[piece], at] = upper[cut]
                low[to : to + widths[piece], at] = lower[cut]

    z = me // 4

    def at_z(steps, act):
        if steps > 0:
            pl.when(z + steps < depth_z)(act)
        else:
            pl.when(z + steps >= 0)(act)

    def send(parity, slot, target, kind, mark, piece):
        return pltpu.make_async_remote_copy(
            src_ref=gathered[parity][piece].at[slot],
            dst_ref=gathered[parity][piece].at[slot],
            send_sem=send_sem.at[kind, mark, piece],
            recv_sem=recv_sem.at[parity, slot, piece],
            device_id={"body": target},
        )

    def wait_in(parity, slot, piece):
        send(parity, slot, flip(me, 1), 0, slot, piece).wait_recv()

    def to_core(parity, slot, piece):
        return send(parity, slot, flip(me, 1), 0, slot, piece)

    def to_row(parity, slot, piece):
        return send(parity, slot, flip(me, 2), 1, slot, piece)

    def own_sends(parity, piece, act):
        for steps in range(1, DIRECT + 1):
            for way in (steps, -steps):
                target = me + 4 * way
                at_z(way, lambda target=target: act(send(parity, me, target, 3, target, piece)))
            if steps == 1:
                act(to_row(parity, me, piece))
        act(to_core(parity, me, piece))

    def column(parity, steps, piece, arrive, act):
        for way in (steps, -steps):
            def one(way=way):
                slot = me + 4 * way
                if arrive:
                    wait_in(parity, slot, piece)
                if steps >= DIRECT:
                    on = -1 if way > 0 else 1
                    at_z(on, lambda: act(send(parity, slot, me + 4 * on, 2, slot, piece)))
                act(to_row(parity, slot, piece))
                act(to_core(parity, slot, piece))
            at_z(way, one)

    def other(parity, steps, piece, arrive, act):
        for way in {steps: None, -steps: None}:
            def one(way=way):
                slot = flip(me, 2) + 4 * way
                if arrive:
                    wait_in(parity, slot, piece)
                act(to_core(parity, slot, piece))
            if way:
                at_z(way, one)
            else:
                one()

    def start(copy):
        copy.start()

    def wait_send(copy):
        copy.wait_send()

    def relay_column(parity, piece):
        for steps in range(1, depth_z):
            column(parity, steps, piece, True, start)
            if steps > 1:
                other(parity, steps - 2, piece, True, start)

    def relay_other(parity, piece):
        for steps in range(max(depth_z - 2, 0), depth_z):
            other(parity, steps, piece, True, start)
        for plane in range(depth_z):
            for row in range(2):
                wait_in(parity, 4 * plane + 2 * row + 1 - me % 2, piece)

    def wait_sends(parity):
        for piece in range(PIECES):
            own_sends(parity, piece, wait_send)
            for steps in range(depth_z):
                if steps:
                    column(parity, steps, piece, False, wait_send)
                other(parity, steps, piece, False, wait_send)

    def solve(parity, value):
        for piece, cut in enumerate(cuts):
            put_field(lhs, 2 * cut.start, value[:, cut], heads)
        for piece, cut in enumerate(cuts):
            part = multiply(lhs, 0, 2 * panels, inv_high, inv_low, cut, rows)
            if parity is None:
                product[:, cut] = part
            else:
                gathered[parity][piece][me] = part
                own_sends(parity, piece, start)

    for part in range(2):
        split(part, inv_high, inv_low, part, 2)
    pl.semaphore_wait(barrier, bodies - 1)
    solve(0, incident[0].reshape(rows, panels))
    for part in range(2 * slots):
        split(2 + part, cross_high, cross_low, part, 2 * slots)

    def sweep(parity):
        for piece in range(PIECES):
            relay_column(parity, piece)
            if piece > 0:
                consume(parity, piece - 1)
        consume(parity, PIECES - 1)
        wait_sends(parity)

    def consume(parity, piece):
        relay_other(parity, piece)
        for slot in range(slots):
            name = neighbours[0, slot]
            value = gathered[parity][piece][jnp.maximum(name, 0)]
            put_field(lhs, 2 * slot * widths[piece], jnp.where(name >= 0, value, 0.0), heads)
        depth = 2 * slots * widths[piece]
        for cut in tiles:
            part = multiply(lhs, 2 * slots * cuts[piece].start, depth, cross_high, cross_low, cut, rows)
            before = incident[0, :, :, cut].reshape(rows, 256) if piece == 0 else product[:, cut]
            product[:, cut] = before - part

    @pl.loop(0, ITERS // 2)
    def _(pair):
        sweep(0)
        solve(1, product[...])
        sweep(1)

        @pl.when(pair < ITERS // 2 - 1)
        def _():
            solve(0, product[...])

    solve(None, product[...])
    final = product[...]
    out[0] = final.reshape(2, heads, panels)
    scale = jnp.broadcast_to(weight[...], (8, panels))
    sums = [
        lax.dot_general(
            scale, final[c * heads : (c + 1) * heads], (((1,), (1,)), ((), ())),
            precision=lax.Precision.HIGHEST, preferred_element_type=F32,
        )
        for c in range(2)
    ]
    row = lax.broadcasted_iota(jnp.int32, (8, heads), 0)
    shares[me] = jnp.zeros((8, 128), F32)
    shares[me, :, 0:heads] = jnp.where(row == 0, sums[0], sums[1])

    def share(bits):
        return pltpu.make_async_remote_copy(
            src_ref=shares.at[me],
            dst_ref=shares.at[me],
            send_sem=share_send.at[bits],
            recv_sem=share_recv.at[bits],
            device_id={"body": flip(me, bits)},
        )

    def share_in(bits):
        slot = flip(me, bits)
        return pltpu.make_async_remote_copy(
            src_ref=shares.at[slot],
            dst_ref=shares.at[slot],
            send_sem=share_send.at[bits],
            recv_sem=share_recv.at[bits],
            device_id={"body": slot},
        )

    for bits in range(1, bodies):
        share(bits).start()
    for bits in range(1, bodies):
        share_in(bits).wait_recv()
    total = shares[0]
    for other in range(1, bodies):
        total = total + shares[other]
    force[0] = total[0:2, 0:heads]
    for bits in range(1, bodies):
        share(bits).wait_send()


def solution(mesh):
    bodies = mesh.shape["body"]

    def step(incident, self_inverse, cross_blocks, neighbours, panel_weight):
        heads, panels = incident.shape[2:]
        slots = neighbours.shape[1]
        rows = 2 * heads
        vmem = pl.BlockSpec(memory_space=pltpu.VMEM)
        anywhere = pl.BlockSpec(memory_space=pl.ANY)
        return pl.pallas_call(
            functools.partial(kernel, bodies, slots, heads, panels),
            out_shape=(
                jax.ShapeDtypeStruct(incident.shape, F32),
                jax.ShapeDtypeStruct((1, 2, heads), F32),
            ),
            in_specs=[pl.BlockSpec(memory_space=pltpu.SMEM), vmem, anywhere, anywhere, vmem],
            out_specs=(vmem, vmem),
            scratch_shapes=[
                pltpu.VMEM((2 + 2 * slots, panels, panels), F32),
                pltpu.VMEM((2 * panels, panels), BF16),
                pltpu.VMEM((2 * panels, panels), BF16),
                pltpu.VMEM((2 * slots * panels, panels), BF16),
                pltpu.VMEM((2 * slots * panels, panels), BF16),
                pltpu.VMEM((2 * rows, 2 * slots * panels), BF16),
                pltpu.VMEM((rows, panels), F32),
                pltpu.VMEM((bodies, 8, 128), F32),
                pltpu.SemaphoreType.DMA((2 + 2 * slots,)),
                pltpu.SemaphoreType.DMA((4, bodies, PIECES)),
                pltpu.SemaphoreType.DMA((2, bodies, PIECES)),
                pltpu.SemaphoreType.DMA((bodies,)),
                pltpu.SemaphoreType.DMA((bodies,)),
                *[pltpu.VMEM((bodies, rows, width), F32) for _, width in pieces(panels)] * 2,
            ],
            compiler_params=pltpu.CompilerParams(
                collective_id=0, has_side_effects=True, vmem_limit_bytes=60 * 1024 * 1024
            ),
        )(neighbours, incident, self_inverse, cross_blocks, panel_weight)

    return jax.shard_map(
        step,
        mesh=mesh,
        in_specs=(
            P(("farm", "body"), None, None, None),
            P(("farm", "body"), None, None, None),
            P(("farm", "body"), None, None, None, None),
            P(("farm", "body"), None),
            P(("farm", "body"), None),
        ),
        out_specs=(P(("farm", "body"), None, None, None), P("farm", None, None)),
        check_vma=False,
    )
```

profile of v0, /device:TPU:1, one launch (start us, length us, event | category | flops | bytes accessed | tf_op | source)
XLA Modules:
  0.0 134.3 jit_solution(14105578589005701184)
XLA Ops:
  0.6 130.8 %shard_map.68 = (f32[1,2,16,768]{3,2,1,0:T(8,128)}, f32[1,2,16]{2,1,0:T(2,128)}) custom-call(s32[1,4]{1,0:T(1,128)} %neighbours.1, f32[1,2,16,768]{3,2,1,0:T(8,128)} %incident.1, f32[1,2,768,768]{3,2,1,0:T(8,128)} %inverse.1, f32[1,4,2,768,768]{4,3,2,1,0:T(8,128)} %blocks.1, f32[1,768]{1,0:T(1,128)} %weight.1), custom_call_target="tpu_custom_call" | custom-call | tf_op jit(solution)/shard_map/pallas_call | solution.py:283
  131.5 1.5 %copy.9 = f32[1,2,16,768]{3,2,1,0:T(8,128)} copy(f32[1,2,16,768]{3,2,1,0:T(8,128)} %get-tuple-element.4) | data formatting | bytes 196608
  133.0 1.2 copy.10
where the time goes:
time: 135 us; the launch traced here: 134 us
  Pallas kernels  131 us (97%)
  local copies, waits for them, and re-layouts  2.78 us (2%)
    pallas_call x1, Pallas kernels, step(): pl.pallas_call(functools.partial(kernel, bodies, slots, heads, panels), o...  131 us
    unnamed x2, local copies, waits for them, and re-layouts  2.78 us

commit v1 on v0

v1 whole, which is shorter than its diff:
```python
import functools

import jax
import jax.numpy as jnp
from jax import lax
from jax.experimental import pallas as pl
from jax.experimental.pallas import tpu as pltpu
from jax.sharding import PartitionSpec as P

ITERS = 6
TILE = 256
VIA = (2,)
F32 = jnp.float32
BF16 = jnp.bfloat16


def flip(index, bits):
    bit = 1
    while bit <= bits:
        if bits & bit:
            index = index + bit - 2 * bit * ((index // bit) % 2)
        bit *= 2
    return index


def differ(first, second, bodies):
    total, bit = 0, 1
    while bit < bodies:
        total = total + bit * (((first // bit) + (second // bit)) % 2)
        bit *= 2
    return total


def halves(value):
    high = value.astype(BF16)
    return high, (value - high.astype(F32)).astype(BF16)


def put_field(lhs, column, value, heads):
    rows, width = value.shape
    high, low = halves(value)
    high_t = jnp.concatenate([-high[heads:], high[:heads]], axis=0)
    low_t = jnp.concatenate([-low[heads:], low[:heads]], axis=0)
    lhs[0:rows, column : column + width] = high
    lhs[rows : 2 * rows, column : column + width] = low
    lhs[0:rows, column + width : column + 2 * width] = high_t
    lhs[rows : 2 * rows, column + width : column + 2 * width] = low_t


def multiply(lhs, base, depth, high, low, at, rows):
    deep = slice(base, base + depth)
    both = jnp.dot(lhs[:, 0:depth], high[deep, at], preferred_element_type=F32)
    small = jnp.dot(lhs[0:rows, 0:depth], low[deep, at], preferred_element_type=F32)
    return both[:rows] + both[rows:] + small


def routes(bodies):
    far = [bit for bit in (2**k for k in range(20)) if 4 <= bit < bodies][::-1]
    masks = sorted(
        {sum(bit for j, bit in enumerate(far) if pick >> j & 1) for pick in range(1, 2 ** len(far))},
        key=lambda mask: (bin(mask).count("1"), -mask),
    )
    return far, masks


def kernel(
    bodies, slots, heads, panels,
    neighbours, incident, inverse, blocks, weight,
    out, force,
    stage, inv_high, inv_low, cross_high, cross_low, lhs, lhs_own, product, shares,
    load_sem, send_sem, recv_sem, share_send, share_recv, *gathered,
):
    rows = 2 * heads
    me = lax.axis_index("body")
    count = panels // TILE
    cuts = [slice(start, start + TILE) for start in range(0, panels, TILE)]
    far, masks = routes(bodies)
    last_side = masks[-1] + 2

    def load(index):
        source = inverse.at[0, index] if index < 2 else blocks.at[0, (index - 2) // 2, (index - 2) % 2]
        return pltpu.make_async_copy(source, stage.at[index], load_sem.at[index])

    for index in range(2):
        load(index).start()

    barrier = pltpu.get_barrier_semaphore()
    for bits in range(1, bodies):
        pl.semaphore_signal(barrier, inc=1, device_id={"body": flip(me, bits)})

    for index in range(2, 2 + 2 * slots):
        load(index).start()

    def split(index, high, low, part, parts):
        load(index).wait()

        @pl.loop(0, panels // 128)
        def _(step):
            at = pl.ds(pl.multiple_of(step * 128, 128), 128)
            upper, lower = halves(stage[index, at, :].T)
            for piece, cut in enumerate(cuts):
                to = parts * cut.start + part * TILE
                high[to : to + TILE, at] = upper[cut]
                low[to : to + TILE, at] = lower[cut]

    def copy(parity, mask, bit, piece):
        return pltpu.make_async_remote_copy(
            src_ref=gathered[parity * count + piece].at[mask],
            dst_ref=gathered[parity * count + piece].at[mask ^ bit],
            send_sem=send_sem.at[bit.bit_length() - 1, mask, piece],
            recv_sem=recv_sem.at[parity, mask ^ bit, piece],
            device_id={"body": flip(me, bit)},
        )

    def wait_in(parity, mask, piece):
        copy(parity, mask ^ 1, 1, piece).wait_recv()

    def onward(mask, piece):
        if mask & 1:
            return []
        if mask & 2:
            return [far[-1], 1] if mask == last_side ^ far[-1] and piece in VIA else [1]
        if mask == last_side ^ 2 and piece in VIA:
            return [1]
        low = mask & -mask if mask else 2**20
        return [bit for bit in far if bit < low] + [2, 1]

    def start(parity, mask, piece):
        for bit in onward(mask, piece):
            copy(parity, mask, bit, piece).start()

    def relay(parity, mask, piece):
        wait_in(parity, mask, piece)
        start(parity, mask, piece)

    def drain(parity, mask):
        for piece in range(count):
            for bit in onward(mask, piece):
                copy(parity, mask, bit, piece).wait_send()

    def solve(parity, value):
        for piece, cut in enumerate(cuts):
            put_field(lhs_own, 2 * cut.start, value[:, cut], heads)
        for piece, cut in enumerate(cuts):
            part = multiply(lhs_own, 0, 2 * panels, inv_high, inv_low, cut, rows)
            if parity is None:
                product[:, cut] = part
            else:
                gathered[parity * count + piece][0] = part
                start(parity, 0, piece)

    names = [neighbours[0, slot] for slot in range(slots)]
    places = [differ(jnp.maximum(name, 0), me, bodies) for name in names]

    def consume(parity, piece):
        for mask in range(1, bodies, 2):
            wait_in(parity, mask, piece)
        for slot in range(slots):
            value = gathered[parity * count + piece][places[slot]]
            put_field(lhs, 2 * slot * TILE, jnp.where(names[slot] >= 0, value, 0.0), heads)
        depth = 2 * slots * TILE
        for cut in cuts:
            part = multiply(lhs, 2 * slots * cuts[piece].start, depth, cross_high, cross_low, cut, rows)
            before = incident[0, :, :, cut].reshape(rows, TILE) if piece == 0 else product[:, cut]
            product[:, cut] = before - part

    for part in range(2):
        split(part, inv_high, inv_low, part, 2)
    pl.semaphore_wait(barrier, bodies - 1)
    solve(0, incident[0].reshape(rows, panels))

    stages = [masks[: len(far)], masks[len(far) :]]
    sides = [mask + 2 for mask in masks]
    sides = [mask for mask in sides if mask == last_side ^ far[-1]] + [2] + [mask for mask in sides if mask != last_side ^ far[-1]]

    def sweep(parity, pair):
        def first(parts):
            if parity == 0:
                @pl.when(pair == 0)
                def _():
                    for part in parts:
                        split(2 + part, cross_high, cross_low, part, 2 * slots)

        total = 2 * slots
        marks = [0, (3 * total) // 8, (6 * total) // 8, total]
        first(range(marks[0], marks[1]))
        for mask in stages[0]:
            for piece in range(count):
                relay(parity, mask, piece)
        first(range(marks[1], marks[2]))
        for mask in stages[1]:
            for piece in range(count):
                relay(parity, mask, piece)
        first(range(marks[2], marks[3]))
        for mask in sides[:-1]:
            for piece in range(count):
                relay(parity, mask, piece)
        drain(parity, 0)
        for mask in stages[0]:
            drain(parity, mask)
        last = sides[-1]
        for piece in range(count):
            relay(parity, last, piece)
        for piece in range(count):
            consume(parity, piece)
        for mask in stages[1] + sides:
            drain(parity, mask)

    @pl.loop(0, ITERS // 2)
    def _(pair):
        sweep(0, pair)
        solve(1, product[...])
        sweep(1, pair)

        @pl.when(pair < ITERS // 2 - 1)
        def _():
            solve(0, product[...])

    solve(None, product[...])
    final = product[...]
    out[0] = final.reshape(2, heads, panels)
    scale = jnp.broadcast_to(weight[...], (8, panels))
    sums = [
        lax.dot_general(
            scale, final[c * heads : (c + 1) * heads], (((1,), (1,)), ((), ())),
            precision=lax.Precision.HIGHEST, preferred_element_type=F32,
        )
        for c in range(2)
    ]
    row = lax.broadcasted_iota(jnp.int32, (8, heads), 0)
    shares[0] = jnp.zeros((8, 128), F32)
    shares[0, :, 0:heads] = jnp.where(row == 0, sums[0], sums[1])

    def share(bits):
        return pltpu.make_async_remote_copy(
            src_ref=shares.at[0],
            dst_ref=shares.at[bits],
            send_sem=share_send.at[bits],
            recv_sem=share_recv.at[bits],
            device_id={"body": flip(me, bits)},
        )

    for bits in range(1, bodies):
        share(bits).start()
    for bits in range(1, bodies):
        share(bits).wait_recv()
    total = jnp.zeros((8, 128), F32)
    for body in range(bodies):
        total = total + shares[differ(me, body, bodies)]
    force[0] = total[0:2, 0:heads]
    for bits in range(1, bodies):
        share(bits).wait_send()


def solution(mesh):
    bodies = mesh.shape["body"]

    def step(incident, self_inverse, cross_blocks, neighbours, panel_weight):
        heads, panels = incident.shape[2:]
        slots = neighbours.shape[1]
        rows = 2 * heads
        count = panels // TILE
        vmem = pl.BlockSpec(memory_space=pltpu.VMEM)
        anywhere = pl.BlockSpec(memory_space=pl.ANY)
        return pl.pallas_call(
            functools.partial(kernel, bodies, slots, heads, panels),
            out_shape=(
                jax.ShapeDtypeStruct(incident.shape, F32),
                jax.ShapeDtypeStruct((1, 2, heads), F32),
            ),
            in_specs=[pl.BlockSpec(memory_space=pltpu.SMEM), vmem, anywhere, anywhere, vmem],
            out_specs=(vmem, vmem),
            scratch_shapes=[
                pltpu.VMEM((2 + 2 * slots, panels, panels), F32),
                pltpu.VMEM((2 * panels, panels), BF16),
                pltpu.VMEM((2 * panels, panels), BF16),
                pltpu.VMEM((2 * slots * panels, panels), BF16),
                pltpu.VMEM((2 * slots * panels, panels), BF16),
                pltpu.VMEM((2 * rows, 2 * slots * TILE), BF16),
                pltpu.VMEM((2 * rows, 2 * panels), BF16),
                pltpu.VMEM((rows, panels), F32),
                pltpu.VMEM((bodies, 8, 128), F32),
                pltpu.SemaphoreType.DMA((2 + 2 * slots,)),
                pltpu.SemaphoreType.DMA((bodies.bit_length(), bodies, count)),
                pltpu.SemaphoreType.DMA((2, bodies, count)),
                pltpu.SemaphoreType.DMA((bodies,)),
                pltpu.SemaphoreType.DMA((bodies,)),
                *[pltpu.VMEM((bodies, rows, TILE), F32)] * (2 * count),
            ],
            compiler_params=pltpu.CompilerParams(
                collective_id=0, has_side_effects=True, vmem_limit_bytes=60 * 1024 * 1024
            ),
        )(neighbours, incident, self_inverse, cross_blocks, panel_weight)

    return jax.shard_map(
        step,
        mesh=mesh,
        in_specs=(
            P(("farm", "body"), None, None, None),
            P(("farm", "body"), None, None, None),
            P(("farm", "body"), None, None, None, None),
            P(("farm", "body"), None),
            P(("farm", "body"), None),
        ),
        out_specs=(P(("farm", "body"), None, None, None), P("farm", None, None)),
        check_vma=False,
    )
```

time: 135 us -> 126 us (0.933)
  Pallas kernels: 131 us -> 122 us
    pallas_call x1, Pallas kernels: 131 us -> 122 us  [step(): pl.pallas_call(functools.partial(kernel, bodies, slots, heads, panels), o...]
where the time goes in v1:
time: 126 us
  Pallas kernels  122 us (97%)
  local copies, waits for them, and re-layouts  2.78 us (2%)
    pallas_call x1, Pallas kernels, step(): pl.pallas_call(functools.partial(kernel, bodies, slots, heads, panels), o...  122 us
    unnamed x2, local copies, waits for them, and re-layouts  2.78 us

profile of v1, /device:TPU:1, one launch (start us, length us, event | category | flops | bytes accessed | tf_op | source)
XLA Modules:
  0.0 125.7 jit_solution(2784629272346507479)
XLA Ops:
  0.6 122.3 %shard_map.68 = (f32[1,2,16,768]{3,2,1,0:T(8,128)}, f32[1,2,16]{2,1,0:T(2,128)}) custom-call(s32[1,4]{1,0:T(1,128)} %neighbours.1, f32[1,2,16,768]{3,2,1,0:T(8,128)} %incident.1, f32[1,2,768,768]{3,2,1,0:T(8,128)} %inverse.1, f32[1,4,2,768,768]{4,3,2,1,0:T(8,128)} %blocks.1, f32[1,768]{1,0:T(1,128)} %weight.1), custom_call_target="tpu_custom_call" | custom-call | tf_op jit(solution)/shard_map/pallas_call | solution.py:265
  122.9 1.5 %copy.9 = f32[1,2,16,768]{3,2,1,0:T(8,128)} copy(f32[1,2,16,768]{3,2,1,0:T(8,128)} %get-tuple-element.4) | data formatting | bytes 196608
  124.5 1.2 copy.10

commit v2 on v1

--- a/solution.py
+++ b/solution.py
@@ -67,7 +67,8 @@
     bodies, slots, heads, panels,
     neighbours, incident, inverse, blocks, weight,
     out, force,
-    stage, inv_high, inv_low, cross_high, cross_low, lhs, lhs_own, product, shares,
+    stage, inv_high, inv_low, cross_high, cross_low, lhs, lhs_own, product, final, shares,
+    scale, sums, pull, tally,
     load_sem, send_sem, recv_sem, share_send, share_recv, *gathered,
 ):
     rows = 2 * heads
@@ -138,98 +139,61 @@
             for bit in onward(mask, piece):
                 copy(parity, mask, bit, piece).wait_send()
 
-    def solve(parity, value):
+    def turn(parity, act):
+        for each in range(2):
+            pl.when(parity == each)(functools.partial(act, each))
+
+    def solve(sweep, parity):
+        value = product[...]
         for piece, cut in enumerate(cuts):
             put_field(lhs_own, 2 * cut.start, value[:, cut], heads)
         for piece, cut in enumerate(cuts):
             part = multiply(lhs_own, 0, 2 * panels, inv_high, inv_low, cut, rows)
-            if parity is None:
-                product[:, cut] = part
-            else:
-                gathered[parity * count + piece][0] = part
-                start(parity, 0, piece)
+            final[:, :, cut] = part.reshape(2, heads, TILE)
+
+            @pl.when(sweep < ITERS)
+            def _():
+                def send(each):
+                    gathered[each * count + piece][0] = part
+                    start(each, 0, piece)
+
+                turn(parity, send)
 
     names = [neighbours[0, slot] for slot in range(slots)]
     places = [differ(jnp.maximum(name, 0), me, bodies) for name in names]
 
-    def consume(parity, piece):
-        for mask in range(1, bodies, 2):
-            wait_in(parity, mask, piece)
-        for slot in range(slots):
-            value = gathered[parity * count + piece][places[slot]]
-            put_field(lhs, 2 * slot * TILE, jnp.where(names[slot] >= 0, value, 0.0), heads)
-        depth = 2 * slots * TILE
-        for cut in cuts:
-            part = multiply(lhs, 2 * slots * cuts[piece].start, depth, cross_high, cross_low, cut, rows)
-            before = incident[0, :, :, cut].reshape(rows, TILE) if piece == 0 else product[:, cut]
-            product[:, cut] = before - part
-
-    for part in range(2):
-        split(part, inv_high, inv_low, part, 2)
-    pl.semaphore_wait(barrier, bodies - 1)
-    solve(0, incident[0].reshape(rows, panels))
-
-    stages = [masks[: len(far)], masks[len(far) :]]
-    sides = [mask + 2 for mask in masks]
-    sides = [mask for mask in sides if mask == last_side ^ far[-1]] + [2] + [mask for mask in sides if mask != last_side ^ far[-1]]
-
-    def sweep(parity, pair):
-        def first(parts):
-            if parity == 0:
-                @pl.when(pair == 0)
-                def _():
-                    for part in parts:
-                        split(2 + part, cross_high, cross_low, part, 2 * slots)
-
-        total = 2 * slots
-        marks = [0, (3 * total) // 8, (6 * total) // 8, total]
-        first(range(marks[0], marks[1]))
-        for mask in stages[0]:
-            for piece in range(count):
-                relay(parity, mask, piece)
-        first(range(marks[1], marks[2]))
-        for mask in stages[1]:
-            for piece in range(count):
-                relay(parity, mask, piece)
-        first(range(marks[2], marks[3]))
-        for mask in sides[:-1]:
-            for piece in range(count):
-                relay(parity, mask, piece)
-        drain(parity, 0)
-        for mask in stages[0]:
-            drain(parity, mask)
-        last = sides[-1]
-        for piece in range(count):
-            relay(parity, last, piece)
-        for piece in range(count):
-            consume(parity, piece)
-        for mask in stages[1] + sides:
-            drain(parity, mask)
-
-    @pl.loop(0, ITERS // 2)
-    def _(pair):
-        sweep(0, pair)
-        solve(1, product[...])
-        sweep(1, pair)
-
-        @pl.when(pair < ITERS // 2 - 1)
-        def _():
-            solve(0, product[...])
-
-    solve(None, product[...])
-    final = product[...]
-    out[0] = final.reshape(2, heads, panels)
-    scale = jnp.broadcast_to(weight[...], (8, panels))
-    sums = [
-        lax.dot_general(
-            scale, final[c * heads : (c + 1) * heads], (((1,), (1,)), ((), ())),
-            precision=lax.Precision.HIGHEST, preferred_element_type=F32,
-        )
-        for c in range(2)
-    ]
-    row = lax.broadcasted_iota(jnp.int32, (8, heads), 0)
-    shares[0] = jnp.zeros((8, 128), F32)
-    shares[0, :, 0:heads] = jnp.where(row == 0, sums[0], sums[1])
+    def set_scale(value):
+        scale[0:8], scale[8:16] = halves(value)
+
+    def weigh(index):
+        sums[...] = jnp.zeros_like(sums)
+
+        @pl.loop(0, count)
+        def _(step):
+            at = pl.ds(pl.multiple_of(step * TILE, TILE), TILE)
+            upper, lower = halves(stage[index, at, :])
+            both = jnp.dot(scale[:, at], upper, preferred_element_type=F32)
+            small = jnp.dot(scale[0:8, at], lower, preferred_element_type=F32)
+            sums[...] += both[0:8] + both[8:16] + small
+
+        return sums[...]
+
+    top = lax.broadcasted_iota(jnp.int32, (8, panels), 0) == 0
+
+    def pulled(slot, value, cut):
+        turned = jnp.concatenate([-value[heads:], value[:heads]], axis=0)
+        return pull[slot, 0:1, cut] * value + pull[slot, 1:2, cut] * turned
+
+    def pull_own():
+        set_scale(jnp.broadcast_to(weight[...], (8, panels)))
+        real = weigh(0)
+        pull[0] = jnp.where(top, real, weigh(1))
+        set_scale(pull[0])
+        tally[...] = pulled(0, incident[0].reshape(rows, panels), slice(0, panels))
+
+    def pull_slot(slot):
+        real, imag = weigh(2 + 2 * slot), weigh(3 + 2 * slot)
+        pull[1 + slot] = jnp.where(top, real[0:1] - imag[1:2], imag[0:1] + real[1:2])
 
     def share(bits):
         return pltpu.make_async_remote_copy(
@@ -240,8 +204,104 @@
             device_id={"body": flip(me, bits)},
         )
 
-    for bits in range(1, bodies):
-        share(bits).start()
+    def arrive(parity, piece):
+        for mask in range(1, bodies, 2):
+            wait_in(parity, mask, piece)
+
+    def held(parity, piece, slot):
+        value = gathered[parity * count + piece][places[slot]]
+        return jnp.where(names[slot] >= 0, value, 0.0)
+
+    LAST = (ITERS - 1) % 2
+
+    def send_share():
+        for piece, cut in enumerate(cuts):
+            arrive(LAST, piece)
+            value = tally[:, cut]
+            for slot in range(slots):
+                value = value - pulled(1 + slot, held(LAST, piece, slot), cut)
+            tally[:, cut] = value
+        ones = jnp.ones((8, panels), F32)
+        real, imag = [
+            lax.dot_general(
+                ones, tally[c * heads : (c + 1) * heads], (((1,), (1,)), ((), ())),
+                precision=lax.Precision.HIGHEST, preferred_element_type=F32,
+            )
+            for c in range(2)
+        ]
+        row = lax.broadcasted_iota(jnp.int32, (8, heads), 0)
+        shares[0] = jnp.zeros((8, 128), F32)
+        shares[0, :, 0:heads] = jnp.where(row == 0, real, imag)
+        for bits in range(1, bodies):
+            share(bits).start()
+
+    def consume(sweep, parity, piece):
+        def take(each):
+            if each == LAST:
+                pl.when(sweep < ITERS - 1)(lambda: arrive(each, piece))
+            else:
+                arrive(each, piece)
+            for slot in range(slots):
+                put_field(lhs, 2 * slot * TILE, held(each, piece, slot), heads)
+
+        turn(parity, take)
+        depth = 2 * slots * TILE
+        for cut in cuts:
+            part = multiply(lhs, 2 * slots * cuts[piece].start, depth, cross_high, cross_low, cut, rows)
+            before = incident[0, :, :, cut].reshape(rows, TILE) if piece == 0 else product[:, cut]
+            product[:, cut] = before - part
+
+    for part in range(2):
+        split(part, inv_high, inv_low, part, 2)
+    pl.semaphore_wait(barrier, bodies - 1)
+    product[...] = incident[0].reshape(rows, panels)
+
+    stages = [masks[: len(far)], masks[len(far) :]]
+    sides = [mask + 2 for mask in masks]
+    sides = [mask for mask in sides if mask == last_side ^ far[-1]] + [2] + [mask for mask in sides if mask != last_side ^ far[-1]]
+
+    def exchange(sweep, parity):
+        def first(parts):
+            @pl.when(sweep == 0)
+            def _():
+                for part in parts:
+                    split(2 + part, cross_high, cross_low, part, 2 * slots)
+
+        def relays(some):
+            def act(each):
+                for mask in some:
+                    for piece in range(count):
+                        relay(each, mask, piece)
+
+            turn(parity, act)
+
+        total = 2 * slots
+        first(range(0, (3 * total) // 8))
+        for slot in range(slots):
+            pl.when(sweep == 1 + slot % (ITERS - 2))(functools.partial(pull_slot, slot))
+        relays(stages[0])
+        first(range((3 * total) // 8, (6 * total) // 8))
+        relays(stages[1])
+        first(range((6 * total) // 8, total))
+        pl.when(sweep == 0)(pull_own)
+        relays(sides[:-1])
+        for mask in [0] + stages[0]:
+            drain(0, mask)
+        relays(sides[-1:])
+        pl.when(sweep == ITERS - 1)(send_share)
+        for piece in range(count):
+            consume(sweep, parity, piece)
+        for mask in stages[1] + sides:
+            drain(0, mask)
+
+    @pl.loop(0, ITERS + 1)
+    def _(sweep):
+        parity = lax.rem(sweep, 2)
+        solve(sweep, parity)
+        pl.when(sweep < ITERS)(lambda: exchange(sweep, parity))
+
+    save = pltpu.make_async_copy(final, out.at[0], load_sem.at[0])
+    save.start()
     for bits in range(1, bodies):
         share(bits).wait_recv()
     total = jnp.zeros((8, 128), F32)
@@ -250,6 +310,7 @@
     force[0] = total[0:2, 0:heads]
     for bits in range(1, bodies):
         share(bits).wait_send()
+    save.wait()
 
 
 def solution(mesh):
@@ -269,7 +330,7 @@
                 jax.ShapeDtypeStruct((1, 2, heads), F32),
             ),
             in_specs=[pl.BlockSpec(memory_space=pltpu.SMEM), vmem, anywhere, anywhere, vmem],
-            out_specs=(vmem, vmem),
+            out_specs=(anywhere, vmem),
             scratch_shapes=[
                 pltpu.VMEM((2 + 2 * slots, panels, panels), F32),
                 pltpu.VMEM((2 * panels, panels), BF16),
@@ -279,7 +340,12 @@
                 pltpu.VMEM((2 * rows, 2 * slots * TILE), BF16),
                 pltpu.VMEM((2 * rows, 2 * panels), BF16),
                 pltpu.VMEM((rows, panels), F32),
+                pltpu.VMEM((2, heads, panels), F32),
                 pltpu.VMEM((bodies, 8, 128), F32),
+                pltpu.VMEM((16, panels), BF16),
+                pltpu.VMEM((8, panels), F32),
+                pltpu.VMEM((1 + slots, 8, panels), F32),
+                pltpu.VMEM((rows, panels), F32),
                 pltpu.SemaphoreType.DMA((2 + 2 * slots,)),
                 pltpu.SemaphoreType.DMA((bodies.bit_length(), bodies, count)),
                 pltpu.SemaphoreType.DMA((2, bodies, count)),

time: 126 us -> 123 us (0.976)
  Pallas kernels: 122 us -> 120 us
    pallas_call x1, Pallas kernels: 122 us -> 120 us  [step(): pl.pallas_call(functools.partial(kernel, bodies, slots, heads, panels), o...]
where the time goes in v2:
time: 123 us
  Pallas kernels  120 us (98%)
  local copies, waits for them, and re-layouts  2.78 us (2%)
    pallas_call x1, Pallas kernels, step(): pl.pallas_call(functools.partial(kernel, bodies, slots, heads, panels), o...  120 us
    unnamed x2, local copies, waits for them, and re-layouts  2.78 us

profile of v2, /device:TPU:1, one launch (start us, length us, event | category | flops | bytes accessed | tf_op | source)
XLA Modules:
  0.0 123.1 jit_solution(3855777349308822661)
XLA Ops:
  0.6 119.6 %shard_map.68 = (f32[1,2,16,768]{3,2,1,0:T(8,128)}, f32[1,2,16]{2,1,0:T(2,128)}) custom-call(s32[1,4]{1,0:T(1,128)} %neighbours.1, f32[1,2,16,768]{3,2,1,0:T(8,128)} %incident.1, f32[1,2,768,768]{3,2,1,0:T(8,128)} %inverse.1, f32[1,4,2,768,768]{4,3,2,1,0:T(8,128)} %blocks.1, f32[1,768]{1,0:T(1,128)} %weight.1), custom_call_target="tpu_custom_call" | custom-call | tf_op jit(solution)/shard_map/pallas_call | solution.py:326
  120.3 1.5 %copy.9 = f32[1,2,16,768]{3,2,1,0:T(8,128)} copy(f32[1,2,16,768]{3,2,1,0:T(8,128)} %get-tuple-element.4) | data formatting | bytes 196608
  121.8 1.2 %copy.10 = f32[1,2,16]{2,1,0:T(2,128)} copy(f32[1,2,16]{2,1,0:T(2,128)} %get-tuple-element.5) | data formatting | bytes 256

commit v3 on v2

--- a/solution.py
+++ b/solution.py
@@ -267,10 +267,10 @@
                 for part in parts:
                     split(2 + part, cross_high, cross_low, part, 2 * slots)
 
-        def relays(some):
+        def relays(some, which=range(count)):
             def act(each):
-                for mask in some:
-                    for piece in range(count):
+                for piece in which:
+                    for mask in some:
                         relay(each, mask, piece)
 
             turn(parity, act)
@@ -287,9 +287,17 @@
         relays(sides[:-1])
         for mask in [0] + stages[0]:
             drain(0, mask)
-        relays(sides[-1:])
-        pl.when(sweep == ITERS - 1)(send_share)
-        for piece in range(count):
+        rear = range(count - 1, count)
+        relays(sides[-1:], range(count - 1))
+
+        @pl.when(sweep == ITERS - 1)
+        def _():
+            relays(sides[-1:], rear)
+            send_share()
+
+        consume(sweep, parity, 0)
+        pl.when(sweep < ITERS - 1)(lambda: relays(sides[-1:], rear))
+        for piece in range(1, count):
             consume(sweep, parity, piece)
         for mask in stages[1] + sides:
             drain(0, mask)

time: 123 us -> 119 us (0.967)
  Pallas kernels: 120 us -> 116 us
    pallas_call x1, Pallas kernels: 120 us -> 116 us  [step(): pl.pallas_call(functools.partial(kernel, bodies, slots, heads, panels), o...]
where the time goes in v3:
time: 119 us
  Pallas kernels  116 us (97%)
  local copies, waits for them, and re-layouts  2.78 us (2%)
    pallas_call x1, Pallas kernels, step(): pl.pallas_call(functools.partial(kernel, bodies, slots, heads, panels), o...  116 us
    unnamed x2, local copies, waits for them, and re-layouts  2.78 us

profile of v3, /device:TPU:1, one launch (start us, length us, event | category | flops | bytes accessed | tf_op | source)
XLA Modules:
  0.0 119.0 jit_solution(16550177733871258979)
XLA Ops:
  0.6 115.6 %shard_map.68 = (f32[1,2,16,768]{3,2,1,0:T(8,128)}, f32[1,2,16]{2,1,0:T(2,128)}) custom-call(s32[1,4]{1,0:T(1,128)} %neighbours.1, f32[1,2,16,768]{3,2,1,0:T(8,128)} %incident.1, f32[1,2,768,768]{3,2,1,0:T(8,128)} %inverse.1, f32[1,4,2,768,768]{4,3,2,1,0:T(8,128)} %blocks.1, f32[1,768]{1,0:T(1,128)} %weight.1), custom_call_target="tpu_custom_call" | custom-call | tf_op jit(solution)/shard_map/pallas_call | solution.py:334
  116.3 1.5 %copy.9 = f32[1,2,16,768]{3,2,1,0:T(8,128)} copy(f32[1,2,16,768]{3,2,1,0:T(8,128)} %get-tuple-element.4) | data formatting | bytes 196608
  117.8 1.2 %copy.10 = f32[1,2,16]{2,1,0:T(2,128)} copy(f32[1,2,16]{2,1,0:T(2,128)} %get-tuple-element.5) | data formatting | bytes 256

commit v4 on v3

--- a/solution.py
+++ b/solution.py
@@ -271,16 +271,21 @@
             def act(each):
                 for piece in which:
                     for mask in some:
-                        relay(each, mask, piece)
+                        wait_in(each, mask, piece)
+                        for bit in onward(mask, piece):
+                            if bit > 1:
+                                copy(each, mask, bit, piece).start()
+                    for mask in some:
+                        copy(each, mask, 1, piece).start()
 
             turn(parity, act)
 
         total = 2 * slots
-        first(range(0, (3 * total) // 8))
+        first(range(0, (4 * total) // 8))
         for slot in range(slots):
             pl.when(sweep == 1 + slot % (ITERS - 2))(functools.partial(pull_slot, slot))
         relays(stages[0])
-        first(range((3 * total) // 8, (6 * total) // 8))
+        first(range((4 * total) // 8, (6 * total) // 8))
         relays(stages[1])
         first(range((6 * total) // 8, total))
         pl.when(sweep == 0)(pull_own)

time: 119 us -> 119 us (level)
  no operation moved by 1% of the time
where the time goes in v4:
time: 119 us
  Pallas kernels  115 us (97%)
  local copies, waits for them, and re-layouts  2.78 us (2%)
    pallas_call x1, Pallas kernels, step(): pl.pallas_call(functools.partial(kernel, bodies, slots, heads, panels), o...  115 us
    unnamed x2, local copies, waits for them, and re-layouts  2.78 us

profile of v4, /device:TPU:1, one launch (start us, length us, event | category | flops | bytes accessed | tf_op | source)
XLA Modules:
  0.0 118.8 jit_solution(13209791483848700344)
XLA Ops:
  0.6 115.4 %shard_map.68 = (f32[1,2,16,768]{3,2,1,0:T(8,128)}, f32[1,2,16]{2,1,0:T(2,128)}) custom-call(s32[1,4]{1,0:T(1,128)} %neighbours.1, f32[1,2,16,768]{3,2,1,0:T(8,128)} %incident.1, f32[1,2,768,768]{3,2,1,0:T(8,128)} %inverse.1, f32[1,4,2,768,768]{4,3,2,1,0:T(8,128)} %blocks.1, f32[1,768]{1,0:T(1,128)} %weight.1), custom_call_target="tpu_custom_call" | custom-call | tf_op jit(solution)/shard_map/pallas_call | solution.py:339
  116.0 1.5 %copy.9 = f32[1,2,16,768]{3,2,1,0:T(8,128)} copy(f32[1,2,16,768]{3,2,1,0:T(8,128)} %get-tuple-element.4) | data formatting | bytes 196608
  117.6 1.2 %copy.10 = f32[1,2,16]{2,1,0:T(2,128)} copy(f32[1,2,16]{2,1,0:T(2,128)} %get-tuple-element.5) | data formatting | bytes 256

commit v5 on v4

--- a/solution.py
+++ b/solution.py
@@ -89,11 +89,11 @@
     for bits in range(1, bodies):
         pl.semaphore_signal(barrier, inc=1, device_id={"body": flip(me, bits)})
 
-    for index in range(2, 2 + 2 * slots):
-        load(index).start()
-
     def split(index, high, low, part, parts):
         load(index).wait()
+        if index == 1:
+            for later in range(2, 2 + 2 * slots):
+                load(later).start()
 
         @pl.loop(0, panels // 128)
         def _(step):

time: 119 us -> 119 us (level)
  no operation moved by 1% of the time
where the time goes in v5:
time: 119 us
  Pallas kernels  115 us (97%)
  local copies, waits for them, and re-layouts  2.78 us (2%)
    pallas_call x1, Pallas kernels, step(): pl.pallas_call(functools.partial(kernel, bodies, slots, heads, panels), o...  115 us
    unnamed x2, local copies, waits for them, and re-layouts  2.78 us

profile of v5, /device:TPU:1, one launch (start us, length us, event | category | flops | bytes accessed | tf_op | source)
XLA Modules:
  0.0 118.8 jit_solution(9240898529083552680)
XLA Ops:
  0.6 115.4 %shard_map.68 = (f32[1,2,16,768]{3,2,1,0:T(8,128)}, f32[1,2,16]{2,1,0:T(2,128)}) custom-call(s32[1,4]{1,0:T(1,128)} %neighbours.1, f32[1,2,16,768]{3,2,1,0:T(8,128)} %incident.1, f32[1,2,768,768]{3,2,1,0:T(8,128)} %inverse.1, f32[1,4,2,768,768]{4,3,2,1,0:T(8,128)} %blocks.1, f32[1,768]{1,0:T(1,128)} %weight.1), custom_call_target="tpu_custom_call" | custom-call | tf_op jit(solution)/shard_map/pallas_call | solution.py:339
  116.1 1.5 %copy.9 = f32[1,2,16,768]{3,2,1,0:T(8,128)} copy(f32[1,2,16,768]{3,2,1,0:T(8,128)} %get-tuple-element.4) | data formatting | bytes 196608
  117.6 1.2 %copy.10 = f32[1,2,16]{2,1,0:T(2,128)} copy(f32[1,2,16]{2,1,0:T(2,128)} %get-tuple-element.5) | data formatting | bytes 256
